TPU v7x, 256 devices: a whole 4x4x8 slice. The times are simulated.
256 devices in a mesh: grp: 8 (over y, core), dev: 32 (over z, x).
Axes of the slice: x: 4, y: 4, z: 8, core: 2. Of those that a mesh axis runs over, the one named last changes fastest.
Arguments:
- sample_rows: bfloat16 [262144, 768], P(('grp', 'dev'))
- row_cell: int32 [262144], P(('grp', 'dev')), may hold values from 0 to 65535, as said below
- tile_rows: int32 [512], P(('grp', 'dev')), may hold values from 0 to 512, as said below
- centroids: bfloat16 [65536, 768], P(('grp', 'dev')), may hold values from -4 to 4
- rotation: bfloat16 [768, 768], replicated, may hold values from -0.21875 to 0.21875
- codebooks: bfloat16 [96, 8, 256], replicated, may hold values from -5 to 5
Outputs:
- cross_cov: float32 [768, 768], replicated
- code_sums: float32 [96, 8, 256], replicated
- code_mass: float32 [96, 256], replicated
Inputs may be any that keep to these rules, and one draw needn't show every extreme that they name: `row_cell`: every row's cell is owned by the device that holds the row: cell // 256 equals row // 1024; cells are unevenly filled. `tile_rows`: the first tile of every device is full; others hold any number of live rows.
All inputs are finite; a program needn't handle non-finite values.
Results may differ from a plain program's by a relative error of at most 0.0024.
Values may be sent and summed in bfloat16 or wider, within the bound.
A program may use at most 64 MiB of HBM per device.

v0:
```python
import jax
import jax.numpy as jnp
from jax import lax
from jax.sharding import PartitionSpec as P

SUB_BLOCK = 8


BETA = 0.5


def prepare(rows, cells, count, centroids, cell_base):
    tile = rows.shape[0]
    valid = (jnp.arange(tile) < count).astype(jnp.float32)
    onehot = ((cells - cell_base)[:, None] == jnp.arange(centroids.shape[0])[None, :]).astype(
        jnp.bfloat16
    )
    cent = jnp.dot(onehot, centroids, preferred_element_type=jnp.float32)
    resid = (rows.astype(jnp.float32) - cent).astype(jnp.bfloat16)
    return (resid, valid)


def statistics(resid, valid, rotation, codebooks):
    tile = resid.shape[0]
    width = resid.shape[1]
    subs = codebooks.shape[0]
    sub_dim = codebooks.shape[1]
    codes = codebooks.shape[2]
    rotated = jnp.dot(resid, rotation, preferred_element_type=jnp.float32).astype(jnp.bfloat16)
    nblk = subs // SUB_BLOCK
    ys = rotated.reshape(tile, nblk, SUB_BLOCK, sub_dim).transpose(1, 0, 2, 3)
    cbs = codebooks.reshape(nblk, SUB_BLOCK, sub_dim, codes)

    def step(carry, pair):
        yb, cb = pair
        cross = jnp.einsum("rmd,mdk->rmk", yb, cb, preferred_element_type=jnp.float32)
        yf = yb.astype(jnp.float32)
        cf = cb.astype(jnp.float32)
        ysq = jnp.sum(yf * yf, -1)[:, :, None]
        csq = jnp.sum(cf * cf, 1)[None]
        score = -BETA * (ysq - 2.0 * cross + csq)
        weight = (jax.nn.softmax(score, -1) * valid[:, None, None]).astype(jnp.bfloat16)
        sums = jnp.einsum("rmk,rmd->mdk", weight, yb, preferred_element_type=jnp.float32)
        mass = jnp.sum(weight.astype(jnp.float32), 0)
        approx = jnp.einsum("rmk,mdk->rmd", weight, cb, preferred_element_type=jnp.float32).astype(
            jnp.bfloat16
        )
        return (carry, (sums, mass, approx))

    unused, (sums, mass, approx) = lax.scan(step, jnp.float32(0.0), (ys, cbs))
    approx = approx.transpose(1, 0, 2, 3).reshape(tile, width)
    cov = lax.dot_general(
        resid, approx, (((0,), (0,)), ((), ())), preferred_element_type=jnp.float32
    )
    return (cov, sums.reshape(subs, sub_dim, codes), mass.reshape(subs, codes))


def per_device(sample_rows, row_cell, tile_rows, centroids, rotation, codebooks):
    n_dev = lax.axis_size("dev")
    n_grp = lax.axis_size("grp")
    device = lax.axis_index("grp") * n_dev + lax.axis_index("dev")
    cells_dev = centroids.shape[0]
    slots = tile_rows.shape[0]
    tile = sample_rows.shape[0] // slots
    width = sample_rows.shape[1]
    cell_base = device * cells_dev
    empty = (
        jnp.zeros((width, width), jnp.float32),
        jnp.zeros(codebooks.shape, jnp.float32),
        jnp.zeros((codebooks.shape[0], codebooks.shape[2]), jnp.float32),
    )
    resids = []
    valids = []
    for slot in range(slots):
        rows = sample_rows[slot * tile : (slot + 1) * tile]
        cells = row_cell[slot * tile : (slot + 1) * tile]
        resid, valid = prepare(rows, cells, tile_rows[slot], centroids, cell_base)
        resids.append(resid)
        valids.append(valid)
    cov, sums, mass = empty
    for slot in range(slots):
        resid = resids[slot]
        valid = valids[slot]

        def work(resid=resid, valid=valid):
            return statistics(resid, valid, rotation, codebooks)

        terms = work()
        cov = cov + terms[0]
        sums = sums + terms[1]
        mass = mass + terms[2]
    cov, sums, mass = lax.psum((cov, sums, mass), ("grp", "dev"))
    total = float(slots * tile * n_dev * n_grp)
    codes = codebooks.shape[2]
    return (cov / total, sums * (codes / total), mass * (codes / total))


def solution(mesh):
    placed = (
        P(("grp", "dev"), None),
        P(("grp", "dev")),
        P(("grp", "dev")),
        P(("grp", "dev"), None),
        P(),
        P(),
    )
    return jax.shard_map(
        per_device, mesh=mesh, in_specs=placed, out_specs=(P(), P(), P()), check_vma=False
    )
```

profile of v0, /device:TPU:1, one launch (start us, length us, event | category | flops | bytes accessed | tf_op | source)
XLA Modules:
  0.0 643.5 jit_solution(15825911352842358833)
XLA Ops:
  13.7 148.0 %while.30 = (s32[]{:T(128)}, f32[12,8,8,256]{3,2,1,0:T(8,128)S(1)}, f32[12,8,256]{2,1,0:T(8,128)}, bf16[12,512,8,8]{1,3,2,0:T(8,128)(2,1)S(1)}, bf16[12,512,8,8]...) while((s32[]{:T(128)}, f32[12,8,8,256]{3,2,1,0:T(8,128)S(1)}, ...), condition=%wide.region_6.7_spmd.clone, body=%wide.region_0.6_spmd.clone.sunk | while | flops 62039296 | bytes 15220321 | solution.py:50
  15.7 4.5 fusion.141
  28.0 4.5 fusion.141
  40.3 4.5 fusion.141
  52.7 4.5 fusion.141
  65.0 4.5 fusion.141
  102.0 4.5 fusion.141
  114.3 4.5 fusion.141
  126.7 4.5 fusion.141
  151.3 4.5 fusion.141
  172.9 183.8 %while.31 = (s32[]{:T(128)}, f32[12,8,8,256]{3,2,1,0:T(8,128)}, f32[12,8,256]{2,1,0:T(8,128)}, bf16[12,512,8,8]{1,3,2,0:T(8,128)(2,1)}, bf16[12,512,8,8]{1,3,2,0...) while((s32[]{:T(128)}, f32[12,8,8,256]{3,2,1,0:T(8,128)}, ...), condition=%wide.region_13.14_spmd.clone, body=%wide.region_7.13_spmd.clone.sunk | while | flops 62039296 | bytes 15220321 | solution.py:50
  175.7 4.6 fusion.151
  191.1 4.6 fusion.151
  206.4 4.6 fusion.151
  221.7 4.6 fusion.151
  237.0 4.6 fusion.151
  252.4 4.6 fusion.151
  267.7 4.6 fusion.151
  283.0 4.6 fusion.151
  298.3 4.6 fusion.151
  313.6 4.6 fusion.151
  329.0 4.6 fusion.151
  344.3 4.6 fusion.151
  363.0 268.7 %all-reduce.3.cloned.1.call-done = (f32[768,768]{1,0:T(8,128)}, f32[96,8,256]{2,1,0:T(8,128)}, f32[96,256]{1,0:T(8,128)}) async-done(((f32[768,768]{1,0:T(8,128)}, f32[96,8,256]{2,1,0:T(8,128)}, f32[96,256]{1,0:T(8,128)}), (f32[768,768]{1,0:T(8,128)}, f32[96,8,256]{2,1,0:T(8,128)}, f32[96,256]{1,0:T(8,128)})) %all-reduce.3.cloned.1.call-update) | async-done | bytes 3244048 | tf_op jit(solution)/shard_map/psum | solution.py:92
  (220 shorter events, 264.7 us)
Async XLA Ops:
  7.2 4.0 copy-start
  7.2 624.5 %all-reduce.3.cloned.1.call-start = ((), (), s32[]{:S(2)}) async-start(), calls=%async_computation | async-start | bytes 6488064 | tf_op jit(solution)/shard_map/psum | solution.py:92
  10.3 0.9 copy-start.7
  11.2 1.1 copy-start.10
  161.6 0.9 copy-start.2
  161.6 1.1 copy-start.4
  161.6 3.4 copy-start.9
  161.6 3.4 copy-start.11
  161.6 3.4 copy-start.12
  165.4 0.9 copy-start.5
  356.7 3.7 copy-start.1
  356.7 3.7 copy-start.3
  631.7 3.3 copy-start.6
  631.7 4.2 copy-start.8
Sparse Core Ops, SparseCore 0:
  363.2 268.5 all-reduce.2
where the time goes:
time: 652 us; the launch traced here: 643 us
  waiting for transfers between devices  269 us (41%)
  matrix products  187 us (29%)
  other arithmetic  149 us (23%)
  local copies, waits for them, and re-layouts  24 us (4%)
  between operations  14.2 us (2%)
    psum x1, waiting for transfers between devices, per_device(): cov, sums, mass = lax.psum((cov, sums, mass), ('grp', 'dev'))  269 us
    sub x24, matrix products, step(): jax.nn.softmax(score, -1) * valid[:, None, None]  109 us
    reduce_sum x24, other arithmetic, step(): mass = jnp.sum(weight.astype(jnp.float32), 0)  66.6 us
    dot_general x24, matrix products, step(): jnp.einsum('rmk,mdk->rmd', weight, cb, preferred_element_type=jnp.float32)  34.8 us
    dot_general x24, matrix products, step(): jnp.einsum('rmk,rmd->mdk', weight, yb, preferred_element_type=jnp.float32)  33.2 us
    reduce_sum x24, other arithmetic, step(): csq = jnp.sum(cf * cf, 1)[None]  33.1 us
    reduce_sum x24, other arithmetic, step(): ysq = jnp.sum(yf * yf, -1)[:, :, None]  25.6 us
    convert_element_type x24, other arithmetic, prepare(): valid = (jnp.arange(tile) < count).astype(jnp.float32)  14.7 us
  transfers between devices with their start and end apart: 1, of which 1 were waited for; matrix products, arithmetic and copies ran while one was open for 0% of the time, Pallas kernels for 0%

commit v1 on v0

v1 whole, which is shorter than its diff:
```python
import functools
from jax.sharding import PartitionSpec as P
import jax
import jax.numpy as jnp
from jax import lax
import jax.experimental.pallas as pl, jax.experimental.pallas.tpu as pltpu
bf=jnp.bfloat16; f32=jnp.float32
LOG2E=1.4426950408889634
NT=(((1,),(1,)),((),()))
TN=(((0,),(0,)),((),()))
R=1024; D=768; K=256; G=6; GM=16
CH=256

def prep(rows,cell,cent,rot,cb,resid,yx,yT):
    for b in range(R//256):
        rs=slice(b*256,(b+1)*256)
        oh=(lax.broadcasted_iota(jnp.int32,(256,256),0)==cell[0:1,rs]).astype(bf)
        c=lax.dot_general(oh,cent[...],TN,preferred_element_type=f32)
        rr=(rows[rs,:].astype(f32)-c).astype(bf)
        resid[rs,:]=rr
        y=jnp.dot(rr,rot[...],preferred_element_type=f32)
        yT[:,rs]=y.T.astype(bf)
        yb=y.astype(bf)
        for g in range(G):
            yx[g,rs,0:128]=yb[:,g*128:(g+1)*128]
            yx[g,rs,128:256]=jnp.ones((256,128),bf)

def score_mat(c, j):
    row=lax.broadcasted_iota(jnp.int32,(128,256),0)
    rep=jnp.concatenate([c]*16,axis=0)
    top=jnp.where(row//8==j,rep,0.0)
    bias=-0.5*jnp.sum(c*c,axis=0,keepdims=True)
    h=bias.astype(bf).astype(f32); r1=bias-h; m=r1.astype(bf).astype(f32); l=r1-m
    bot=jnp.where(row==0,h,jnp.where(row==1,m,jnp.where(row==2,l,0.0)))
    return jnp.concatenate([top,bot],axis=0).astype(bf)

def stage1(g,j,cb,yx,E,mode):
    c=cb[g*GM+j].astype(f32)
    A=score_mat(c,j)
    for ch in range(R//CH):
        rs=slice(ch*CH,(ch+1)*CH)
        s=jnp.dot(yx[g,rs,:],A,preferred_element_type=f32)
        if mode=="max":
            s=s-jnp.max(s,axis=1,keepdims=True)
        E[rs,:]=jnp.exp2(s*LOG2E).astype(bf)

def stage2(g,j,cb,yT,E,valid,apT,sums,mass,held):
    c=cb[g*GM+j].astype(f32)
    one=(lax.broadcasted_iota(jnp.int32,(8,256),0)==0).astype(f32)
    caug=jnp.concatenate([c,one],axis=0).astype(bf)
    q=lax.dot_general(caug,E[...],NT,preferred_element_type=f32)
    inv=valid/q[8:9,:]
    ap=q[0:8,:]*inv
    r0=pl.multiple_of(g*128+(j//2)*16,16)
    y16=yT[pl.ds(r0,16),:].astype(f32)
    ym=y16[(j%2)*8:(j%2)*8+8,:]
    rowid=lax.broadcasted_iota(jnp.int32,(8,R),0)
    L=jnp.concatenate([ym*inv,jnp.where(rowid==0,inv,0.0)],axis=0).astype(bf)
    o=jnp.dot(L,E[...],preferred_element_type=f32)
    sums[g*GM+j]=o[0:8,:]
    held.append((ap,o[8:9,:]))
    if j%2==1:
        apT[pl.ds(r0,16),:]=jnp.concatenate([held[-2][0],held[-1][0]],axis=0).astype(bf)
    if j%8==7:
        mass[pl.ds(pl.multiple_of(g*16+j-7,8),8),:]=jnp.concatenate([h[1] for h in held[-8:]],axis=0)

def kernel(mode,tiles,rows,cell,cent,rot,cb,cov,sums,mass,resid,yx,yT,apT,*Es):
    prep(rows,cell,cent,rot,cb,resid,yx,yT)
    pos=lax.broadcasted_iota(jnp.int32,(1,R),1)
    valid=(pos<jnp.where(pos<512,tiles[0],512+tiles[1])).astype(f32)
    NE=len(Es)
    def body(g,_):
        held=[]
        stage1(g,0,cb,yx,Es[0],mode)
        for j in range(GM):
            if j+1<GM: stage1(g,j+1,cb,yx,Es[(j+1)%NE],mode)
            stage2(g,j,cb,yT,Es[j%NE],valid,apT,sums,mass,held)
        return 0
    lax.fori_loop(0,G,body,0)
    for i in range(3):
        cs=slice(i*256,(i+1)*256)
        cov[:,cs]=lax.dot_general(resid[...],apT[cs,:],(((0,),(1,)),((),())),preferred_element_type=f32)

def run(mode,NE,tiles,rows,cell,cent,rot,cb):
    V=pl.BlockSpec(memory_space=pltpu.VMEM)
    S=jax.ShapeDtypeStruct
    return pl.pallas_call(functools.partial(kernel,mode),
      out_shape=(S((D,D),f32),S((96,8,256),f32),S((96,256),f32)),
      in_specs=[pl.BlockSpec(memory_space=pltpu.SMEM)]+[V]*5,out_specs=(V,V,V),
      scratch_shapes=[pltpu.VMEM((R,D),bf),pltpu.VMEM((G,R,256),bf),pltpu.VMEM((D,R),bf),pltpu.VMEM((D,R),bf)]+[pltpu.VMEM((R,256),bf)]*NE,
      compiler_params=pltpu.CompilerParams(vmem_limit_bytes=60*2**20))(tiles,rows,cell,cent,rot,cb)


def per_device(sample_rows, row_cell, tile_rows, centroids, rotation, codebooks):
    n_dev = lax.axis_size("dev")
    n_grp = lax.axis_size("grp")
    device = lax.axis_index("grp") * n_dev + lax.axis_index("dev")
    cell = (row_cell - device * centroids.shape[0]).reshape(1, R)
    cov, sums, mass = run("max", 2, tile_rows, sample_rows, cell, centroids, rotation, codebooks)
    cov, sums, mass = lax.psum((cov, sums, mass), ("grp", "dev"))
    total = float(R * n_dev * n_grp)
    return cov / total, sums * (K / total), mass * (K / total)


def solution(mesh):
    placed = (P(("grp", "dev"), None), P(("grp", "dev")), P(("grp", "dev")), P(("grp", "dev"), None), P(), P())
    return jax.shard_map(per_device, mesh=mesh, in_specs=placed, out_specs=(P(), P(), P()), check_vma=False)
```

time: 652 us -> 331 us (0.51); the launches traced: 643 us -> 330 us
  matrix products: 187 us -> 0 us
  other arithmetic: 149 us -> 6.17 us
  Pallas kernels: 0 us -> 41.3 us
  local copies, waits for them, and re-layouts: 24 us -> 0.01 us
    reduce_sum x72 -> x0, other arithmetic: 125 us -> none  [the longest x24 66.6 us: step(): mass = jnp.sum(weight.astype(jnp.float32), 0)]
    sub x24 -> x0, matrix products: 109 us -> none  [step(): jax.nn.softmax(score, -1) * valid[:, None, None]]
    dot_general x54 -> x0, matrix products: 78.4 us -> none  [the longest x24 34.8 us: step(): jnp.einsum('rmk,mdk->rmd', weight, cb, preferred_element_type=jnp.float32)]
    pallas_call x0 -> x1, Pallas kernels: none -> 41.3 us  [run(): pl.pallas_call(functools.partial(kernel, mode), out_shape=(S((D, D), f32)...]
    convert_element_type x24 -> x0, other arithmetic: 14.7 us -> none  [prepare(): valid = (jnp.arange(tile) < count).astype(jnp.float32)]
    dynamic_update_slice x24 -> x0, local copies, waits for them, and re-layouts: 14.5 us -> none  [statistics(): unused, (sums, mass, approx) = lax.scan(step, jnp.float32(0.0), (ys, cbs))]
where the time goes in v1:
time: 331 us; the launch traced here: 330 us
  waiting for transfers between devices  268 us (81%)
  Pallas kernels  41.3 us (12%)
  between operations  14 us (4%)
  other arithmetic  6.17 us (2%)
    psum x1, waiting for transfers between devices, per_device(): cov, sums, mass = lax.psum((cov, sums, mass), ('grp', 'dev'))  268 us
    pallas_call x1, Pallas kernels, run(): pl.pallas_call(functools.partial(kernel, mode), out_shape=(S((D, D), f32)...  41.3 us
  transfers between devices with their start and end apart: 1, of which 1 were waited for; matrix products, arithmetic and copies ran while one was open for 0% of the time, Pallas kernels for 0%

profile of v1, /device:TPU:1, one launch (start us, length us, event | category | flops | bytes accessed | tf_op | source)
XLA Modules:
  0.0 329.9 jit_solution(3729049711428341748)
XLA Ops:
  7.2 0.0 all-reduce.3.cloned.1.call-start
  7.2 1.3 broadcast_subtract_fusion
  8.5 41.3 %shard_map.85 = (f32[768,768]{1,0:T(8,128)}, f32[96,8,256]{2,1,0:T(8,128)}, f32[96,256]{1,0:T(8,128)}) custom-call(s32[2]{0:T(128)} %tiles.1, bf16[1024,768]{1,0:T(8,128)(2,1)} %rows.1, s32[1,1024]{1,0:T(1,128)} %bitcast.1, bf16[256,768]{1,0:T(8,128)(2,1)} %cent.1, bf16[768,768]{1,0:T(8,128)(2,1)} %rot.1, bf16[96,8,256]{2,1,0:T(8,128)(2,1)} %cb.1), custom_call_target="tpu_custom_call" | custom-call | tf_op jit(solution)/shard_map/pallas_call | solution.py:87
  49.8 0.0 all-reduce.3.cloned.1.call-update
  49.9 268.3 %all-reduce.3.cloned.1.call-done = (f32[768,768]{1,0:T(8,128)}, f32[96,8,256]{2,1,0:T(8,128)}, f32[96,256]{1,0:T(8,128)}) async-done(((f32[768,768]{1,0:T(8,128)}, f32[96,8,256]{2,1,0:T(8,128)}, f32[96,256]{1,0:T(8,128)}), (f32[768,768]{1,0:T(8,128)}, f32[96,8,256]{2,1,0:T(8,128)}, f32[96,256]{1,0:T(8,128)})) %all-reduce.3.cloned.1.call-update) | async-done | bytes 3244048 | tf_op jit(solution)/shard_map/psum | solution.py:100
  318.2 0.0 copy-start.1
  318.2 0.0 copy-start
  318.2 3.3 %broadcast_multiply_fusion = f32[768,768]{1,0:T(8,128)} fusion(f32[768,768]{1,0:T(8,128)} %get-tuple-element.9), kind=kLoop, calls=%fused_computation | loop fusion | flops 589824 | bytes 4718592 | tf_op jit(solution)/shard_map/div | solution.py:102
  321.5 0.0 copy-done.1
  321.5 0.6 broadcast_multiply_fusion.2
  322.2 0.0 copy-done
  322.2 0.9 broadcast_multiply_fusion.1
Async XLA Ops:
  7.2 311.0 %all-reduce.3.cloned.1.call-start = ((), (), s32[]{:S(2)}) async-start(), calls=%async_computation | async-start | bytes 6488064 | tf_op jit(solution)/shard_map/psum | solution.py:100
  318.2 3.3 %copy-start.1 = (f32[96,256]{1,0:T(8,128)S(1)}, f32[96,256]{1,0:T(8,128)}, u32[]{:S(2)}) copy-start(f32[96,256]{1,0:T(8,128)} %get-tuple-element.11) | copy-start | bytes 294916
  318.2 4.0 %copy-start = (f32[96,8,256]{2,1,0:T(8,128)S(1)}, f32[96,8,256]{2,1,0:T(8,128)}, u32[]{:S(2)}) copy-start(f32[96,8,256]{2,1,0:T(8,128)} %get-tuple-element.10) | copy-start | bytes 2359300
Sparse Core Ops, SparseCore 0:
  50.0 268.1 all-reduce.2

commit v2 on v1

v2 whole, which is shorter than its diff:
```python
import functools
from jax.sharding import PartitionSpec as P
import jax
import jax.numpy as jnp
from jax import lax
import jax.experimental.pallas as pl, jax.experimental.pallas.tpu as pltpu
bf=jnp.bfloat16; f32=jnp.float32
LOG2E=1.4426950408889634
NT=(((1,),(1,)),((),()))
TN=(((0,),(0,)),((),()))
R=1024; D=768; K=256; G=6; GM=16
CH=256

def prep(rows,cell,cent,rot,residT,yx,yT):
    for b in range(R//256):
        rs=slice(b*256,(b+1)*256)
        oh=(lax.broadcasted_iota(jnp.int32,(256,256),0)==cell[0:1,rs]).astype(bf)
        c=lax.dot_general(oh,cent[...],TN,preferred_element_type=f32)
        rr=(rows[rs,:].astype(f32)-c).astype(bf)
        residT[:,rs]=rr.astype(f32).T.astype(bf)
        y=jnp.dot(rr,rot[...],preferred_element_type=f32)
        yT[:,rs]=y.T.astype(bf)
        yb=y.astype(bf)
        for g in range(G):
            yx[g,rs,0:128]=yb[:,g*128:(g+1)*128]
            yx[g,rs,128:256]=jnp.ones((256,128),bf)

def score_mat(c, j):
    row=lax.broadcasted_iota(jnp.int32,(128,256),0)
    rep=jnp.concatenate([c]*16,axis=0)
    top=jnp.where(row//8==j,rep,0.0)
    bias=-0.5*jnp.sum(c*c,axis=0,keepdims=True)
    h=bias.astype(bf).astype(f32); r1=bias-h; m=r1.astype(bf).astype(f32); l=r1-m
    bot=jnp.where(row==0,h,jnp.where(row==1,m,jnp.where(row==2,l,0.0)))
    return jnp.concatenate([top,bot],axis=0).astype(bf)

def stage1(g,j,cb,yx,E,mode):
    c=cb[g*GM+j].astype(f32)
    A=score_mat(c,j)
    for ch in range(R//CH):
        rs=slice(ch*CH,(ch+1)*CH)
        s=jnp.dot(yx[g,rs,:],A,preferred_element_type=f32)
        if mode=="max":
            s=s-jnp.max(s,axis=1,keepdims=True)
        E[rs,:]=jnp.exp2(s*LOG2E).astype(bf)


NX=4; NY=4; NZ=8


def stage2(g,j,cb,yT,E,valid,apT,part,held):
    c=cb[g*GM+j].astype(f32)
    one=(lax.broadcasted_iota(jnp.int32,(8,256),0)==0).astype(f32)
    caug=jnp.concatenate([c,one],axis=0).astype(bf)
    q=lax.dot_general(caug,E[...],NT,preferred_element_type=f32)
    inv=valid/q[8:9,:]
    ap=q[0:8,:]*inv
    r0=pl.multiple_of(g*128+(j//2)*16,16)
    ym=yT[pl.ds(r0,16),:].astype(f32)[(j%2)*8:(j%2)*8+8,:]
    rowid=lax.broadcasted_iota(jnp.int32,(8,R),0)
    L=jnp.concatenate([ym*inv,jnp.where(rowid==0,inv,0.0)],axis=0).astype(bf)
    o=jnp.dot(L,E[...],preferred_element_type=f32)
    cc,hh,aa=j//8,(j//4)%2,j%4
    part[g,cc,hh,aa*8+6]=o[0:8,0:128]
    part[g,cc,hh,aa*8+7]=o[0:8,128:256]
    held.append((ap,o[8:9,:]))
    if j%2==1:
        apT[(j//2)*16:(j//2)*16+16,:]=jnp.concatenate([held[-2][0],held[-1][0]],axis=0).astype(bf)
    if j%8==7:
        mm=jnp.concatenate([h[1] for h in held[-8:]],axis=0)
        part[g,cc,0,32]=mm[:,0:128]
        part[g,cc,1,32]=mm[:,128:256]


def covariance(g,residT,apT,part):
    for cc in range(2):
        for hh in range(2):
            i0=cc*384+hh*192
            v=lax.dot_general(residT[i0:i0+192,:],apT[...],NT,preferred_element_type=f32)
            v=v.reshape(4,6,8,128)
            for aa in range(4):
                part[g,cc,hh,aa*8:aa*8+6]=v[aa]


def kernel(tiles,rows,cell,cent,rot,cb,cov,sums,mass,
           residT,yx,yT,apT,E0,E1,part,rc,sa,ra,sz,rz,rl,out,
           s_core,r_core,s_a,r_a,s_z,r_z,s_l,r_l,s_gz,r_gz,s_ga,r_ga,s_gc,r_gc):
    grp=lax.axis_index("grp"); dev=lax.axis_index("dev")
    yy=grp//2; c=lax.rem(grp,2); zz=dev//NX; xx=lax.rem(dev,NX)
    sib=(yy*2+1-c,dev)
    def at_y(t): return (t*2+c,dev)
    def at_x(t): return (grp,zz*NX+t)
    def at_z(t): return (grp,t*NX+xx)
    first=((yy,at_y),(xx,at_x)); last=((xx,at_x),(yy,at_y))

    barrier=pltpu.get_barrier_semaphore()
    peers=[sib]+[at_y(lax.rem(yy+k,NY)) for k in range(1,NY)]+[at_x(lax.rem(xx+k,NX)) for k in range(1,NX)]+[at_z(lax.rem(zz+k,NZ)) for k in range(1,NZ)]
    for p in peers:
        pl.semaphore_signal(barrier,inc=1,device_id=p,device_id_type=pl.DeviceIdType.MESH)

    def copy(src,dst,ss,rs,to):
        return pltpu.make_async_remote_copy(src_ref=src,dst_ref=dst,send_sem=ss,recv_sem=rs,device_id=to,device_id_type=pl.DeviceIdType.MESH)

    def step(k,g):
        if k==0:
            copy(part.at[g,1-c],rc.at[g],s_core.at[0],r_core.at[g],sib).start()
        if k==1:
            copy(rc.at[g],rc.at[g],s_core.at[0],r_core.at[g],sib).wait_recv()
            for h in range(2):
                me,at=first[h]
                tot=part[g,c,h]+rc[g,h]
                for a in range(4):
                    sa[g,h,a,0:8]=tot[a*8:a*8+8]
                    sa[g,h,a,8]=tot[32]
                for kk in range(1,4):
                    a=lax.rem(me+kk,4)
                    copy(sa.at[g,h,a],ra.at[g,h,me],s_a.at[0],r_a.at[g,h],at(a)).start()
                ra[g,h,me]=sa[g,h,me]
        if k==2:
            for h in range(2):
                me,at=first[h]
                copy(sa.at[g,h,0:3],ra.at[g,h,0:3],s_a.at[0],r_a.at[g,h],sib).wait_recv()
                tot=(ra[g,h,0]+ra[g,h,1])+(ra[g,h,2]+ra[g,h,3])
                for z in range(NZ):
                    sz[g,h,z,0]=tot[z]
                    sz[g,h,z,1]=tot[8]
                for kk in range(1,NZ):
                    z=lax.rem(zz+kk,NZ)
                    copy(sz.at[g,h,z],rz.at[g,h,zz],s_z.at[0],r_z.at[g,h],at_z(z)).start()
                rz[g,h,zz]=sz[g,h,zz]
        if k==3:
            for h in range(2):
                me,at=last[h]
                copy(sz.at[g,h,0:7],rz.at[g,h,0:7],s_z.at[0],r_z.at[g,h],sib).wait_recv()
                t=[rz[g,h,z] for z in range(NZ)]
                rl[g,h,me]=((t[0]+t[1])+(t[2]+t[3]))+((t[4]+t[5])+(t[6]+t[7]))
                for kk in range(1,4):
                    a=lax.rem(me+kk,4)
                    copy(rl.at[g,h,me],rl.at[g,h,me],s_l.at[0],r_l.at[g,h],at(a)).start()
        if k==4:
            for h in range(2):
                me,_=first[h]
                copy(rl.at[g,h,0:3],rl.at[g,h,0:3],s_l.at[0],r_l.at[g,h],sib).wait_recv()
                tot=(rl[g,h,0]+rl[g,h,1])+(rl[g,h,2]+rl[g,h,3])
                mine=out.at[g,c,h,me*8+zz]
                mine[...]=tot[0]
                out[g,c,h,32]=tot[1]
                for kk in range(1,NZ):
                    z=lax.rem(zz+kk,NZ)
                    copy(mine,mine,s_gz.at[0],r_gz.at[g,h],at_z(z)).start()
        if k==5:
            for h in range(2):
                me,at=first[h]
                copy(out.at[g,c,h,0:7],out.at[g,c,h,0:7],s_gz.at[0],r_gz.at[g,h],sib).wait_recv()
                mine=out.at[g,c,h,pl.ds(me*8,8)]
                for kk in range(1,4):
                    a=lax.rem(me+kk,4)
                    copy(mine,mine,s_ga.at[0],r_ga.at[g,h],at(a)).start()
        if k==6:
            for h in range(2):
                copy(out.at[g,c,h,0:24],out.at[g,c,h,0:24],s_ga.at[0],r_ga.at[g,h],sib).wait_recv()
            copy(out.at[g,c],out.at[g,c],s_gc.at[0],r_gc.at[g],sib).start()
        if k==7:
            copy(out.at[g,1-c],out.at[g,1-c],s_gc.at[0],r_gc.at[g],sib).wait_recv()
            for cc in range(2):
                for hh in range(2):
                    for aa in range(4):
                        i0=cc*384+hh*192+aa*48
                        cov[i0:i0+48,pl.ds(pl.multiple_of(g*128,128),128)]=out[g,cc,hh,aa*8:aa*8+6].reshape(48,128)
                        for w in range(2):
                            sums[g*GM+cc*8+hh*4+aa,:,w*128:(w+1)*128]=out[g,cc,hh,aa*8+6+w]
                    mass[pl.ds(pl.multiple_of(g*GM+cc*8,8),8),hh*128:(hh+1)*128]=out[g,cc,hh,32]

    prep(rows,cell,cent,rot,residT,yx,yT)
    pos=lax.broadcasted_iota(jnp.int32,(1,R),1)
    valid=(pos<jnp.where(pos<512,tiles[0],512+tiles[1])).astype(f32)
    pl.semaphore_wait(barrier,len(peers))
    Es=(E0,E1)

    def body(g,_):
        held=[]
        stage1(g,0,cb,yx,E0,"max")
        for j in range(GM):
            if j+1<GM: stage1(g,j+1,cb,yx,Es[(j+1)%2],"max")
            stage2(g,j,cb,yT,Es[j%2],valid,apT,part,held)
            if j==7:
                for k in (1,3,5,7):
                    back=(k+1)//2
                    @pl.when(g>=back)
                    def _(k=k,back=back): step(k,g-back)
        covariance(g,residT,apT,part)
        for k in (0,2,4,6):
            back=k//2
            if back==0: step(0,g)
            else:
                @pl.when(g>=back)
                def _(k=k,back=back): step(k,g-back)
        return 0
    lax.fori_loop(0,G,body,0)
    for sp in range(2*G,2*G+7):
        for k in range(8):
            if (sp-1-k)%2==0 and 0<=(sp-1-k)//2<G:
                step(k,(sp-1-k)//2)
    copy(rc,rc,s_core.at[0],r_core.at[0],sib).wait_send()
    copy(sa.at[:,:,0:3],ra.at[:,:,0:3],s_a.at[0],r_a.at[0,0],sib).wait_send()
    copy(sz.at[:,:,0:7],rz.at[:,:,0:7],s_z.at[0],r_z.at[0,0],sib).wait_send()
    copy(rl.at[:,:,0:3],rl.at[:,:,0:3],s_l.at[0],r_l.at[0,0],sib).wait_send()
    copy(out.at[:,0,:,0:7],out.at[:,0,:,0:7],s_gz.at[0],r_gz.at[0,0],sib).wait_send()
    copy(out.at[:,0,:,0:24],out.at[:,0,:,0:24],s_ga.at[0],r_ga.at[0,0],sib).wait_send()
    copy(out.at[:,0],out.at[:,0],s_gc.at[0],r_gc.at[0],sib).wait_send()


def run(tiles,rows,cell,cent,rot,cb):
    V=pl.BlockSpec(memory_space=pltpu.VMEM)
    S=jax.ShapeDtypeStruct
    T=lambda *n: pltpu.VMEM(n+(8,128),f32)
    DS=pltpu.SemaphoreType.DMA
    return pl.pallas_call(kernel,
      out_shape=(S((D,D),f32),S((96,8,256),f32),S((96,256),f32)),
      in_specs=[pl.BlockSpec(memory_space=pltpu.SMEM)]+[V]*5,out_specs=(V,V,V),
      scratch_shapes=[pltpu.VMEM((D,R),bf),pltpu.VMEM((G,R,256),bf),pltpu.VMEM((D,R),bf),pltpu.VMEM((128,R),bf),
                      pltpu.VMEM((R,256),bf),pltpu.VMEM((R,256),bf),
                      T(G,2,2,33),T(G,2,33),T(G,2,4,9),T(G,2,4,9),T(G,2,8,2),T(G,2,8,2),T(G,2,4,2),T(G,2,2,33),
                      DS((1,)),DS((G,)),DS((1,)),DS((G,2)),DS((1,)),DS((G,2)),DS((1,)),DS((G,2)),
                      DS((1,)),DS((G,2)),DS((1,)),DS((G,2)),DS((1,)),DS((G,))],
      compiler_params=pltpu.CompilerParams(vmem_limit_bytes=56*2**20,collective_id=0,has_side_effects=True),
      cost_estimate=pl.CostEstimate(flops=2**34,bytes_accessed=2**23,transcendentals=2**24))(tiles,rows,cell,cent,rot,cb)


def per_device(sample_rows, row_cell, tile_rows, centroids, rotation, codebooks):
    n_dev = lax.axis_size("dev")
    n_grp = lax.axis_size("grp")
    device = lax.axis_index("grp") * n_dev + lax.axis_index("dev")
    cell = (row_cell - device * centroids.shape[0]).reshape(1, R)
    cov, sums, mass = run(tile_rows, sample_rows, cell, centroids, rotation, codebooks)
    total = float(R * n_dev * n_grp)
    return cov / total, sums * (K / total), mass * (K / total)


def solution(mesh):
    placed = (P(("grp", "dev"), None), P(("grp", "dev")), P(("grp", "dev")), P(("grp", "dev"), None), P(), P())
    return jax.shard_map(per_device, mesh=mesh, in_specs=placed, out_specs=(P(), P(), P()), check_vma=False)
```

time: 331 us -> 100 us (0.30)
  waiting for transfers between devices: 268 us -> 0 us
  Pallas kernels: 41.3 us -> 93.4 us
  between operations: 14 us -> 0.66 us
    psum x1 -> x0, waiting for transfers between devices: 268 us -> none  [per_device(): cov, sums, mass = lax.psum((cov, sums, mass), ('grp', 'dev'))]
    pallas_call x1, Pallas kernels: 41.3 us -> 93.4 us  [run(): pl.pallas_call(kernel, out_shape=(S((D, D), f32), S((96, 8, 256), f32), S...]
  transfers between devices with their start and end apart: 1 -> 0, of which waited for: 1 -> 0; matrix products, arithmetic and copies ran while one was open for 0% -> 0% of each run, Pallas kernels for 0% -> 0%
where the time goes in v2:
time: 100 us
  Pallas kernels  93.4 us (93%)
  other arithmetic  6.16 us (6%)
    pallas_call x1, Pallas kernels, run(): pl.pallas_call(kernel, out_shape=(S((D, D), f32), S((96, 8, 256), f32), S...  93.4 us
    div x1, other arithmetic, per_device(): return (cov / total, sums * (K / total), mass * (K / total))  3.3 us

profile of v2, /device:TPU:1, one launch (start us, length us, event | category | flops | bytes accessed | tf_op | source)
XLA Modules:
  0.0 100.3 jit_solution(455229863312393799)
XLA Ops:
  0.6 1.3 %broadcast_subtract_fusion = s32[1024]{0:T(1024)} fusion(s32[1024]{0:T(1024)} %param.7, s32[]{:T(128)S(6)} %mul.19), kind=kLoop, calls=%fused_computation.3 | loop fusion | flops 1024 | bytes 8196 | tf_op jit(solution)/shard_map/sub | solution.py:234
  1.9 93.4 %shard_map.85 = (f32[768,768]{1,0:T(8,128)}, f32[96,8,256]{2,1,0:T(8,128)}, f32[96,256]{1,0:T(8,128)}) custom-call(s32[2]{0:T(128)} %tiles.1, bf16[1024,768]{1,0:T(8,128)(2,1)} %rows.1, s32[1,1024]{1,0:T(1,128)} %bitcast.1, bf16[256,768]{1,0:T(8,128)(2,1)} %cent.1, bf16[768,768]{1,0:T(8,128)(2,1)} %rot.1, bf16[96,8,256]{2,1,0:T(8,128)(2,1)} %cb.1), custom_call_target="tpu_custom_call" | custom-call | flops 17179869184 | bytes 8388608 | tf_op jit(solution)/shard_map/pallas_call | solution.py:218
  95.4 0.0 copy-start.1
  95.4 0.0 copy-start
  95.4 3.3 %broadcast_multiply_fusion = f32[768,768]{1,0:T(8,128)} fusion(f32[768,768]{1,0:T(8,128)} %get-tuple-element.6), kind=kLoop, calls=%fused_computation | loop fusion | flops 589824 | bytes 4718592 | tf_op jit(solution)/shard_map/div | solution.py:237
  98.7 0.0 copy-done.1
  98.7 0.6 broadcast_multiply_fusion.2
  99.3 0.0 copy-done
  99.3 0.9 broadcast_multiply_fusion.1
Async XLA Ops:
  95.4 3.3 %copy-start.1 = (f32[96,256]{1,0:T(8,128)S(1)}, f32[96,256]{1,0:T(8,128)}, u32[]{:S(2)}) copy-start(f32[96,256]{1,0:T(8,128)} %get-tuple-element.8) | copy-start | bytes 294916
  95.4 4.0 %copy-start = (f32[96,8,256]{2,1,0:T(8,128)S(1)}, f32[96,8,256]{2,1,0:T(8,128)}, u32[]{:S(2)}) copy-start(f32[96,8,256]{2,1,0:T(8,128)} %get-tuple-element.7) | copy-start | bytes 2359300

commit v3 on v0

v3 whole, which is shorter than its diff:
```python
import functools
import jax
import jax.numpy as jnp
from jax import lax
from jax.sharding import PartitionSpec as P
import jax.experimental.pallas as pl
import jax.experimental.pallas.tpu as pltpu

bf = jnp.bfloat16
f32 = jnp.float32
LOG2E = 1.4426950408889634
NT = (((1,), (1,)), ((), ()))
TN = (((0,), (0,)), ((), ()))
MESH = pl.DeviceIdType.MESH
R = 1024
D = 768
K = 256
G = 6
GM = 16
CH = 256
NC = R // CH
DB, DC, SLOTS = 5, 10, 12
NX, NY, NZ, NA = 4, 4, 8, 16
ROWS = 262144


def prep(rows, cells, base, cent, rot, wait_rot, residT, yx, yT):
    for b in range(NC):
        rs = slice(b * 256, (b + 1) * 256)
        hot = [
            (lax.broadcasted_iota(jnp.int32, (K, 128), 0) + base == cells[b * 2 + i : b * 2 + i + 1, :]).astype(bf)
            for i in range(2)
        ]
        c = lax.dot_general(jnp.concatenate(hot, axis=1), cent[...], TN, preferred_element_type=f32)
        resid = (rows[rs, :].astype(f32) - c).astype(bf)
        residT[:, rs] = resid.T
        if b == 0:
            wait_rot()
        y = jnp.dot(resid, rot[...], preferred_element_type=f32).astype(bf)
        yT[:, rs] = y.T
        for g in range(G):
            yx[g, rs, :] = y[:, g * 128 : (g + 1) * 128]


def group(g, cb, yx, yT, slots, valid, apT, part, pm, middle):
    U = GM * NC
    mats, lhs, held, sums, mrows = {}, {}, {}, {}, []

    def scores(u):
        j, ch = divmod(u, NC)
        rs = slice(ch * CH, (ch + 1) * CH)
        if ch == 0:
            c = cb[g * GM + j].astype(f32)
            bias = -0.5 * jnp.sum(c * c, axis=0, keepdims=True)
            row = lax.broadcasted_iota(jnp.int32, (128, K), 0)
            mat = jnp.where(row // 8 == j, jnp.concatenate([c] * 16, axis=0), 0.0).astype(bf)
            one = (lax.broadcasted_iota(jnp.int32, (8, K), 0) == 0).astype(f32)
            mats[j] = (mat, jnp.concatenate([c, one], axis=0).astype(bf), bias)
        s = jnp.dot(yx[g, rs, :], mats[j][0], preferred_element_type=f32) + mats[j][2]
        s = s - jnp.max(s, axis=1, keepdims=True)
        slots[u % SLOTS][...] = jnp.exp2(s * LOG2E).astype(bf)

    def reconstruct(u):
        j, ch = divmod(u, NC)
        rs = slice(ch * CH, (ch + 1) * CH)
        q = lax.dot_general(mats[j][1], slots[u % SLOTS][...], NT, preferred_element_type=f32)
        inv = valid[:, rs] / q[8:9, :]
        held[j, ch] = q[0:8, :] * inv
        r0 = pl.multiple_of(g * 128 + (j // 2) * 16, 16)
        y = yT[pl.ds(r0, 16), rs].astype(f32)[(j % 2) * 8 : (j % 2) * 8 + 8, :]
        row = lax.broadcasted_iota(jnp.int32, (8, CH), 0)
        lhs[u] = jnp.concatenate([y * inv, jnp.where(row == 0, inv, 0.0)], axis=0).astype(bf)
        if j % 2 == 1:
            both = [held.pop((j - 1, ch)), held.pop((j, ch))]
            apT[(j // 2) * 16 : (j // 2) * 16 + 16, rs] = jnp.concatenate(both, axis=0).astype(bf)

    def accumulate(u):
        j, ch = divmod(u, NC)
        o = jnp.dot(lhs.pop(u), slots[u % SLOTS][...], preferred_element_type=f32)
        sums[j] = o if ch == 0 else sums[j] + o
        if ch == NC - 1:
            o = sums.pop(j)
            cc, a = j // 8, (j % 8) * 2
            part[g, cc, a, 3] = o[0:8, 0:128]
            part[g, cc, a + 1, 3] = o[0:8, 128:256]
            mrows.append(o[8:9, :])
            if j % 8 == 7:
                m = jnp.concatenate(mrows[-8:], axis=0)
                pm[0, g * 2 + cc] = m[:, 0:128]
                pm[1, g * 2 + cc] = m[:, 128:256]

    for t in range(U + DC):
        if t == U // 2:
            middle()
        if t < U:
            scores(t)
        if 0 <= t - DB < U:
            reconstruct(t - DB)
        if 0 <= t - DC < U:
            accumulate(t - DC)


def covariance(g, residT, apT, part):
    for cc in range(2):
        for hh in range(2):
            i0 = cc * 384 + hh * 192
            v = lax.dot_general(residT[i0 : i0 + 192, :], apT[...], NT, preferred_element_type=f32)
            part[g, cc, hh * 8 : hh * 8 + 8, 0:3] = v.reshape(8, 3, 8, 128)


def kernel(tiles, rows, cells, cent, rot_hbm, cb_hbm, cov_hbm, sums_hbm, mass_hbm,
           rot, cb, cov, sums, mass, residT, yx, yT, apT, part, pm, rc, rcm, sa, ra, rz, out,
           s_in, s_out, s_core, r_core, s_m, r_m, s_a, r_a, s_z, r_z, s_g, r_g, s_c, r_c, *slots):
    grp = lax.axis_index("grp")
    dev = lax.axis_index("dev")
    yy = grp // 2
    c = lax.rem(grp, 2)
    zz = dev // NX
    xx = lax.rem(dev, NX)
    me = yy * NX + xx
    sib = (yy * 2 + 1 - c, dev)

    def plane(a):
        return ((a // NX) * 2 + c, zz * NX + lax.rem(a, NX))

    def column(z):
        return (grp, z * NX + xx)

    others = [lax.rem(me + k, NA) for k in range(1, NA)]
    above = [lax.rem(zz + k, NZ) for k in range(1, NZ)]
    barrier = pltpu.get_barrier_semaphore()
    peers = [sib] + [plane(a) for a in others] + [column(z) for z in above]
    for p in peers:
        pl.semaphore_signal(barrier, inc=1, device_id=p, device_id_type=MESH)

    def copy(src, dst, ss, rs, to):
        return pltpu.make_async_remote_copy(
            src_ref=src, dst_ref=dst, send_sem=ss, recv_sem=rs, device_id=to, device_id_type=MESH
        )

    def size(last):
        return (5, 48) if last else (4, 32)

    def to_out(g):
        cols = pl.ds(pl.multiple_of(g * 128, 128), 128)
        subs = pl.ds(pl.multiple_of(g * GM, GM), GM)
        return (
            pltpu.make_async_copy(cov.at[:, cols], cov_hbm.at[:, cols], s_out.at[0, g]),
            pltpu.make_async_copy(sums.at[subs], sums_hbm.at[subs], s_out.at[1, g]),
        )

    def step(k, g, last=False):
        n, nb = size(last)
        if k == 0:
            copy(part.at[g, 1 - c], rc.at[g], s_core.at[g], r_core.at[g], sib).start()
            if last:
                copy(pm.at[1 - c], rcm, s_m.at[0], r_m.at[0], sib).start()
        if k == 1:
            copy(rc.at[g], rc.at[g], s_core.at[g], r_core.at[g], sib).wait_recv()
            if last:
                copy(rcm, rcm, s_m.at[0], r_m.at[0], sib).wait_recv()
                tot = (pm[c] + rcm[...]).reshape(NA, 8, 128)
                tot = jnp.concatenate([tot, jnp.zeros((NA, 8, 128), f32)], axis=1)
                sa[g, :, 32:48] = tot.astype(bf)
            tot = (part[g, c] + rc[g]).reshape(NA, 32, 128)
            sa[g, :, 0:32] = tot.astype(bf)
            for a in others:
                copy(sa.at[g, a, 0:nb], ra.at[g, me, 0:nb], s_a.at[g], r_a.at[g], plane(a)).start()
            ra[g, me, 0:nb] = sa[g, me, 0:nb]
        if k == 2:
            copy(sa.at[g, 0:15, 0:nb], ra.at[g, 0:15, 0:nb], s_a.at[g], r_a.at[g], sib).wait_recv()
            t = [ra[g, a, 0:nb].astype(f32) for a in range(NA)]
            while len(t) > 1:
                t = [t[i] + t[i + 1] for i in range(0, len(t), 2)]
            rz[g, zz, 0:n] = t[0][0 : n * 8].reshape(n, 8, 128)
            for z in above:
                copy(rz.at[g, zz, 0:n], rz.at[g, zz, 0:n], s_z.at[g], r_z.at[g], column(z)).start()
        if k == 3:
            copy(rz.at[g, 0:7, 0:n], rz.at[g, 0:7, 0:n], s_z.at[g], r_z.at[g], sib).wait_recv()
            t = [rz[g, z, 0:n] for z in range(NZ)]
            while len(t) > 1:
                t = [t[i] + t[i + 1] for i in range(0, len(t), 2)]
            mine = out.at[g, c, me, 0:n]
            mine[...] = t[0]
            for a in others:
                copy(mine, mine, s_g.at[g], r_g.at[g], plane(a)).start()
        if k == 4:
            copy(out.at[g, c, 0:15, 0:n], out.at[g, c, 0:15, 0:n], s_g.at[g], r_g.at[g], sib).wait_recv()
            half = out.at[g, c, :, 0:n]
            copy(half, half, s_c.at[g], r_c.at[g], sib).start()
        if k == 5:
            half = out.at[g, 1 - c, :, 0:n]
            copy(half, half, s_c.at[g], r_c.at[g], sib).wait_recv()
            for cc in range(2):
                i0 = cc * 384
                v = out[g, cc, :, 0:3].reshape(384, 128) * (1.0 / ROWS)
                cov[i0 : i0 + 384, pl.ds(pl.multiple_of(g * 128, 128), 128)] = v
                for a in range(NA):
                    w = a % 2
                    sums[g * GM + cc * 8 + a // 2, :, w * 128 : (w + 1) * 128] = out[g, cc, a, 3] * (K / ROWS)
                if last:
                    for a in range(12):
                        mass[a * 8 : a * 8 + 8, cc * 128 : (cc + 1) * 128] = out[g, cc, a, 4] * (K / ROWS)
            for cp in to_out(g):
                cp.start()

    get_rot = pltpu.make_async_copy(rot_hbm, rot, s_in.at[0])
    get_cb = pltpu.make_async_copy(cb_hbm, cb, s_in.at[1])
    get_rot.start()
    get_cb.start()
    pm[...] = jnp.zeros_like(pm)
    prep(rows, cells, (grp * (NX * NZ) + dev) * K, cent, rot, get_rot.wait, residT, yx, yT)
    pos = lax.broadcasted_iota(jnp.int32, (1, R), 1)
    valid = (pos < jnp.where(pos < 512, tiles[0], 512 + tiles[1])).astype(f32)
    get_cb.wait()

    def when(g, back, k):
        @pl.when(g >= back)
        def _():
            step(k, g - back)

    def body(g, _):
        def middle():
            @pl.when(g == 0)
            def _():
                pl.semaphore_wait(barrier, len(peers))

            when(g, 1, 1)
            when(g, 2, 2)
            when(g, 5, 4)

        group(g, cb, yx, yT, slots, valid, apT, part, pm, middle)
        covariance(g, residT, apT, part)
        step(0, g)
        when(g, 3, 3)
        when(g, 5, 5)
        return 0

    lax.fori_loop(0, G, body, 0)
    copy(pm.at[1 - c], rcm, s_m.at[0], r_m.at[0], sib).start()
    order = ((1, 5), (4, 1), (2, 4), (3, 3), (2, 5), (5, 1), (4, 2), (3, 4), (5, 2), (4, 3), (3, 5), (5, 3), (4, 4), (5, 4), (4, 5), (5, 5))
    for k, g in order:
        step(k, g, g == G - 1)
    put_mass = pltpu.make_async_copy(mass, mass_hbm, s_in.at[0])
    put_mass.start()
    copy(rcm, rcm, s_m.at[0], r_m.at[0], sib).wait_send()
    for g in range(G):
        n, nb = size(g == G - 1)
        copy(rc.at[g], rc.at[g], s_core.at[g], r_core.at[g], sib).wait_send()
        copy(sa.at[g, 0:15, 0:nb], ra.at[g, 0:15, 0:nb], s_a.at[g], r_a.at[g], sib).wait_send()
        copy(rz.at[g, 0:7, 0:n], rz.at[g, 0:7, 0:n], s_z.at[g], r_z.at[g], sib).wait_send()
        copy(out.at[g, 0, 0:15, 0:n], out.at[g, 0, 0:15, 0:n], s_g.at[g], r_g.at[g], sib).wait_send()
        copy(out.at[g, 0, :, 0:n], out.at[g, 0, :, 0:n], s_c.at[g], r_c.at[g], sib).wait_send()
        for cp in to_out(g):
            cp.wait()
    put_mass.wait()


def run(tiles, rows, cells, cent, rot, cb):
    V = pl.BlockSpec(memory_space=pltpu.VMEM)
    A = pl.BlockSpec(memory_space=pl.ANY)
    S = jax.ShapeDtypeStruct
    VM = pltpu.VMEM
    DS = pltpu.SemaphoreType.DMA

    def T(*n):
        return VM(n + (8, 128), f32)

    return pl.pallas_call(
        kernel,
        out_shape=(S((D, D), f32), S((96, 8, K), f32), S((96, K), f32)),
        in_specs=[pl.BlockSpec(memory_space=pltpu.SMEM), V, V, V, A, A],
        out_specs=(A, A, A),
        scratch_shapes=[
            VM((D, D), bf), VM((96, 8, K), bf), VM((D, D), f32), VM((96, 8, K), f32), VM((96, K), f32),
            VM((D, R), bf), VM((G, R, 128), bf), VM((D, R), bf), VM((128, R), bf),
            T(G, 2, NA, 4), T(2, NA), T(G, NA, 4), T(NA),
            VM((G, NA, 48, 128), bf), VM((G, NA, 48, 128), bf), T(G, NZ, 5), T(G, 2, NA, 5),
            DS((2,)), DS((2, G)), DS((G,)), DS((G,)), DS((1,)), DS((1,)), DS((G,)), DS((G,)),
            DS((G,)), DS((G,)), DS((G,)), DS((G,)), DS((G,)), DS((G,)),
        ] + [VM((CH, K), bf)] * SLOTS,
        compiler_params=pltpu.CompilerParams(vmem_limit_bytes=56 * 2**20, collective_id=0, has_side_effects=True),
        cost_estimate=pl.CostEstimate(flops=2**34, bytes_accessed=2**23, transcendentals=2**24),
    )(tiles, rows, cells, cent, rot, cb)


def per_device(sample_rows, row_cell, tile_rows, centroids, rotation, codebooks):
    return run(tile_rows, sample_rows, row_cell.reshape(8, 128), centroids, rotation, codebooks)


def solution(mesh):
    placed = (P(("grp", "dev"), None), P(("grp", "dev")), P(("grp", "dev")), P(("grp", "dev"), None), P(), P())
    return jax.shard_map(
        per_device, mesh=mesh, in_specs=placed, out_specs=(P(), P(), P()), check_vma=False
    )
```

time: 652 us -> 77.1 us (0.12); the launches traced: 643 us -> 76.9 us
  waiting for transfers between devices: 269 us -> 0 us
  matrix products: 187 us -> 0 us
  other arithmetic: 149 us -> 0 us
  Pallas kernels: 0 us -> 71.4 us
  local copies, waits for them, and re-layouts: 24 us -> 4.83 us
  between operations: 14.2 us -> 0.66 us
    psum x1 -> x0, waiting for transfers between devices: 269 us -> none  [per_device(): cov, sums, mass = lax.psum((cov, sums, mass), ('grp', 'dev'))]
    reduce_sum x72 -> x0, other arithmetic: 125 us -> none  [the longest x24 66.6 us: step(): mass = jnp.sum(weight.astype(jnp.float32), 0)]
    sub x24 -> x0, matrix products: 109 us -> none  [step(): jax.nn.softmax(score, -1) * valid[:, None, None]]
    dot_general x54 -> x0, matrix products: 78.4 us -> none  [the longest x24 34.8 us: step(): jnp.einsum('rmk,mdk->rmd', weight, cb, preferred_element_type=jnp.float32)]
    pallas_call x0 -> x1, Pallas kernels: none -> 71.4 us  [run(): pl.pallas_call(kernel, out_shape=(S((D, D), f32), S((96, 8, K), f32), S((...]
    convert_element_type x24 -> x0, other arithmetic: 14.7 us -> none  [prepare(): valid = (jnp.arange(tile) < count).astype(jnp.float32)]
    dynamic_update_slice x24 -> x0, local copies, waits for them, and re-layouts: 14.5 us -> none  [statistics(): unused, (sums, mass, approx) = lax.scan(step, jnp.float32(0.0), (ys, cbs))]
  transfers between devices with their start and end apart: 1 -> 0, of which waited for: 1 -> 0; matrix products, arithmetic and copies ran while one was open for 0% -> 0% of each run, Pallas kernels for 0% -> 0%
where the time goes in v3:
time: 77.1 us; the launch traced here: 76.9 us
  Pallas kernels  71.4 us (93%)
  local copies, waits for them, and re-layouts  4.83 us (6%)
    pallas_call x1, Pallas kernels, run(): pl.pallas_call(kernel, out_shape=(S((D, D), f32), S((96, 8, K), f32), S((...  71.4 us
    unnamed x7, local copies, waits for them, and re-layouts  4.83 us

profile of v3, /device:TPU:1, one launch (start us, length us, event | category | flops | bytes accessed | tf_op | source)
XLA Modules:
  0.0 76.9 jit_solution(1664673381562540288)
XLA Ops:
  0.6 71.4 %shard_map.85 = (f32[768,768]{1,0:T(8,128)}, f32[96,8,256]{2,1,0:T(8,128)}, f32[96,256]{1,0:T(8,128)}) custom-call(s32[2]{0:T(128)} %tiles.1, bf16[1024,768]{1,0:T(8,128)(2,1)} %rows.1, s32[8,128]{1,0:T(8,128)} %bitcast.1, bf16[256,768]{1,0:T(8,128)(2,1)} %cent.1, bf16[768,768]{1,0:T(8,128)(2,1)} %rot_hbm.1, bf16[96,8,256]{2,1,0:T(8,128)(2,1)} %cb_hbm.1), custom_call_target="tpu_custom_call" | custom-call | flops 17179869184 | bytes 8388608 | tf_op jit(solution)/shard_map/pallas_call | solution.py:269
  72.1 0.0 copy-start
  72.1 0.0 copy-start.1
  72.1 3.3 %copy.12 = f32[768,768]{1,0:T(8,128)} copy(f32[768,768]{1,0:T(8,128)} %get-tuple-element.6) | data formatting | bytes 4718592
  75.4 0.0 copy-done
  75.4 0.9 %copy.13 = f32[96,8,256]{2,1,0:T(8,128)} copy(f32[96,8,256]{2,1,0:T(8,128)S(1)} %copy-done) | data formatting | bytes 1572864
  76.3 0.0 copy-done.1
  76.3 0.6 copy.14
Async XLA Ops:
  72.1 3.3 %copy-start = (f32[96,8,256]{2,1,0:T(8,128)S(1)}, f32[96,8,256]{2,1,0:T(8,128)}, u32[]{:S(2)}) copy-start(f32[96,8,256]{2,1,0:T(8,128)} %get-tuple-element.7) | copy-start | bytes 2359300
  72.1 4.2 %copy-start.1 = (f32[96,256]{1,0:T(8,128)S(1)}, f32[96,256]{1,0:T(8,128)}, u32[]{:S(2)}) copy-start(f32[96,256]{1,0:T(8,128)} %get-tuple-element.8) | copy-start | bytes 294916

commit v4 on v3

--- a/solution.py
+++ b/solution.py
@@ -19,12 +19,16 @@
 GM = 16
 CH = 256
 NC = R // CH
-DB, DC, SLOTS = 5, 10, 12
+CHB = 512
+NCB = R // CHB
+PB = CHB // CH
+DB, DC, SLOTS = 6, 12, 6
 NX, NY, NZ, NA = 4, 4, 8, 16
 ROWS = 262144
-
-
-def prep(rows, cells, base, cent, rot, wait_rot, residT, yx, yT):
+VL = 52
+
+
+def prep(rows, cells, base, cent, rot, rows_of, wait_rot, resid, yx, yT):
     for b in range(NC):
         rs = slice(b * 256, (b + 1) * 256)
         hot = [
@@ -32,11 +36,12 @@
             for i in range(2)
         ]
         c = lax.dot_general(jnp.concatenate(hot, axis=1), cent[...], TN, preferred_element_type=f32)
-        resid = (rows[rs, :].astype(f32) - c).astype(bf)
-        residT[:, rs] = resid.T
+        rows_of(b).wait()
+        r = (rows[rs, :].astype(f32) - c).astype(bf)
+        resid[rs, :] = r
         if b == 0:
             wait_rot()
-        y = jnp.dot(resid, rot[...], preferred_element_type=f32).astype(bf)
+        y = jnp.dot(r, rot[...], preferred_element_type=f32).astype(bf)
         yT[:, rs] = y.T
         for g in range(G):
             yx[g, rs, :] = y[:, g * 128 : (g + 1) * 128]
@@ -58,27 +63,28 @@
             mats[j] = (mat, jnp.concatenate([c, one], axis=0).astype(bf), bias)
         s = jnp.dot(yx[g, rs, :], mats[j][0], preferred_element_type=f32) + mats[j][2]
         s = s - jnp.max(s, axis=1, keepdims=True)
-        slots[u % SLOTS][...] = jnp.exp2(s * LOG2E).astype(bf)
+        slots[j % SLOTS][rs, :] = jnp.exp2(s * LOG2E).astype(bf)
 
     def reconstruct(u):
-        j, ch = divmod(u, NC)
-        rs = slice(ch * CH, (ch + 1) * CH)
-        q = lax.dot_general(mats[j][1], slots[u % SLOTS][...], NT, preferred_element_type=f32)
+        j, ch = divmod(u, NCB)
+        rs = slice(ch * CHB, (ch + 1) * CHB)
+        q = lax.dot_general(mats[j][1], slots[j % SLOTS][rs, :], NT, preferred_element_type=f32)
         inv = valid[:, rs] / q[8:9, :]
         held[j, ch] = q[0:8, :] * inv
         r0 = pl.multiple_of(g * 128 + (j // 2) * 16, 16)
         y = yT[pl.ds(r0, 16), rs].astype(f32)[(j % 2) * 8 : (j % 2) * 8 + 8, :]
-        row = lax.broadcasted_iota(jnp.int32, (8, CH), 0)
+        row = lax.broadcasted_iota(jnp.int32, (8, CHB), 0)
         lhs[u] = jnp.concatenate([y * inv, jnp.where(row == 0, inv, 0.0)], axis=0).astype(bf)
         if j % 2 == 1:
             both = [held.pop((j - 1, ch)), held.pop((j, ch))]
             apT[(j // 2) * 16 : (j // 2) * 16 + 16, rs] = jnp.concatenate(both, axis=0).astype(bf)
 
     def accumulate(u):
-        j, ch = divmod(u, NC)
-        o = jnp.dot(lhs.pop(u), slots[u % SLOTS][...], preferred_element_type=f32)
+        j, ch = divmod(u, NCB)
+        rs = slice(ch * CHB, (ch + 1) * CHB)
+        o = jnp.dot(lhs.pop(u), slots[j % SLOTS][rs, :], preferred_element_type=f32)
         sums[j] = o if ch == 0 else sums[j] + o
-        if ch == NC - 1:
+        if ch == NCB - 1:
             o = sums.pop(j)
             cc, a = j // 8, (j % 8) * 2
             part[g, cc, a, 3] = o[0:8, 0:128]
@@ -94,23 +100,21 @@
             middle()
         if t < U:
             scores(t)
-        if 0 <= t - DB < U:
-            reconstruct(t - DB)
-        if 0 <= t - DC < U:
-            accumulate(t - DC)
-
-
-def covariance(g, residT, apT, part):
+        if 0 <= t - DB < U and (t - DB) % PB == PB - 1:
+            reconstruct((t - DB) // PB)
+        if 0 <= t - DC < U and (t - DC) % PB == PB - 1:
+            accumulate((t - DC) // PB)
+
+
+def covariance(g, resid, apT, part):
+    v = jnp.dot(apT[...], resid[...], preferred_element_type=f32)
     for cc in range(2):
-        for hh in range(2):
-            i0 = cc * 384 + hh * 192
-            v = lax.dot_general(residT[i0 : i0 + 192, :], apT[...], NT, preferred_element_type=f32)
-            part[g, cc, hh * 8 : hh * 8 + 8, 0:3] = v.reshape(8, 3, 8, 128)
-
-
-def kernel(tiles, rows, cells, cent, rot_hbm, cb_hbm, cov_hbm, sums_hbm, mass_hbm,
-           rot, cb, cov, sums, mass, residT, yx, yT, apT, part, pm, rc, rcm, sa, ra, rz, out,
-           s_in, s_out, s_core, r_core, s_m, r_m, s_a, r_a, s_z, r_z, s_g, r_g, s_c, r_c, *slots):
+        part[g, cc, :, 0:3] = v[:, cc * 384 : cc * 384 + 384].T.reshape(NA, 3, 8, 128)
+
+
+def kernel(tiles, cells, rows_hbm, cent_hbm, rot_hbm, cb_hbm, cov, sums, mass,
+           rows, cent, rot, cb, resid, yx, yT, apT, part, pm, rc, rcm, sa, ra, rz, out,
+           s_in, s_core, r_core, s_m, r_m, s_a, r_a, s_z, r_z, s_g, r_g, s_c, r_c, *slots):
     grp = lax.axis_index("grp")
     dev = lax.axis_index("dev")
     yy = grp // 2
@@ -128,11 +132,6 @@
 
     others = [lax.rem(me + k, NA) for k in range(1, NA)]
     above = [lax.rem(zz + k, NZ) for k in range(1, NZ)]
-    barrier = pltpu.get_barrier_semaphore()
-    peers = [sib] + [plane(a) for a in others] + [column(z) for z in above]
-    for p in peers:
-        pl.semaphore_signal(barrier, inc=1, device_id=p, device_id_type=MESH)
-
     def copy(src, dst, ss, rs, to):
         return pltpu.make_async_remote_copy(
             src_ref=src, dst_ref=dst, send_sem=ss, recv_sem=rs, device_id=to, device_id_type=MESH
@@ -140,14 +139,6 @@
 
     def size(last):
         return (5, 48) if last else (4, 32)
-
-    def to_out(g):
-        cols = pl.ds(pl.multiple_of(g * 128, 128), 128)
-        subs = pl.ds(pl.multiple_of(g * GM, GM), GM)
-        return (
-            pltpu.make_async_copy(cov.at[:, cols], cov_hbm.at[:, cols], s_out.at[0, g]),
-            pltpu.make_async_copy(sums.at[subs], sums_hbm.at[subs], s_out.at[1, g]),
-        )
 
     def step(k, g, last=False):
         n, nb = size(last)
@@ -201,15 +192,24 @@
                 if last:
                     for a in range(12):
                         mass[a * 8 : a * 8 + 8, cc * 128 : (cc + 1) * 128] = out[g, cc, a, 4] * (K / ROWS)
-            for cp in to_out(g):
-                cp.start()
-
+
+    barrier = pltpu.get_barrier_semaphore()
+    peers = [sib] + [plane(a) for a in others] + [column(z) for z in above]
+    for p in peers:
+        pl.semaphore_signal(barrier, inc=1, device_id=p, device_id_type=MESH)
+
+    def rows_of(b):
+        rs = slice(b * 256, (b + 1) * 256)
+        return pltpu.make_async_copy(rows_hbm.at[rs], rows.at[rs], s_in.at[3 + b])
+
+    get_cent = pltpu.make_async_copy(cent_hbm, cent, s_in.at[2])
     get_rot = pltpu.make_async_copy(rot_hbm, rot, s_in.at[0])
     get_cb = pltpu.make_async_copy(cb_hbm, cb, s_in.at[1])
-    get_rot.start()
-    get_cb.start()
+    for cp in [get_cent, rows_of(0), get_rot] + [rows_of(b) for b in range(1, NC)] + [get_cb]:
+        cp.start()
     pm[...] = jnp.zeros_like(pm)
-    prep(rows, cells, (grp * (NX * NZ) + dev) * K, cent, rot, get_rot.wait, residT, yx, yT)
+    get_cent.wait()
+    prep(rows, cells, (grp * (NX * NZ) + dev) * K, cent, rot, rows_of, get_rot.wait, resid, yx, yT)
     pos = lax.broadcasted_iota(jnp.int32, (1, R), 1)
     valid = (pos < jnp.where(pos < 512, tiles[0], 512 + tiles[1])).astype(f32)
     get_cb.wait()
@@ -230,7 +230,7 @@
             when(g, 5, 4)
 
         group(g, cb, yx, yT, slots, valid, apT, part, pm, middle)
-        covariance(g, residT, apT, part)
+        covariance(g, resid, apT, part)
         step(0, g)
         when(g, 3, 3)
         when(g, 5, 5)
@@ -241,8 +241,6 @@
     order = ((1, 5), (4, 1), (2, 4), (3, 3), (2, 5), (5, 1), (4, 2), (3, 4), (5, 2), (4, 3), (3, 5), (5, 3), (4, 4), (5, 4), (4, 5), (5, 5))
     for k, g in order:
         step(k, g, g == G - 1)
-    put_mass = pltpu.make_async_copy(mass, mass_hbm, s_in.at[0])
-    put_mass.start()
     copy(rcm, rcm, s_m.at[0], r_m.at[0], sib).wait_send()
     for g in range(G):
         n, nb = size(g == G - 1)
@@ -251,15 +249,11 @@
         copy(rz.at[g, 0:7, 0:n], rz.at[g, 0:7, 0:n], s_z.at[g], r_z.at[g], sib).wait_send()
         copy(out.at[g, 0, 0:15, 0:n], out.at[g, 0, 0:15, 0:n], s_g.at[g], r_g.at[g], sib).wait_send()
         copy(out.at[g, 0, :, 0:n], out.at[g, 0, :, 0:n], s_c.at[g], r_c.at[g], sib).wait_send()
-        for cp in to_out(g):
-            cp.wait()
-    put_mass.wait()
 
 
 def run(tiles, rows, cells, cent, rot, cb):
     V = pl.BlockSpec(memory_space=pltpu.VMEM)
-    A = pl.BlockSpec(memory_space=pl.ANY)
-    S = jax.ShapeDtypeStruct
+    A = pl.BlockSpec(memory_space=pltpu.HBM)
     VM = pltpu.VMEM
     DS = pltpu.SemaphoreType.DMA
 
@@ -268,20 +262,20 @@
 
     return pl.pallas_call(
         kernel,
-        out_shape=(S((D, D), f32), S((96, 8, K), f32), S((96, K), f32)),
-        in_specs=[pl.BlockSpec(memory_space=pltpu.SMEM), V, V, V, A, A],
-        out_specs=(A, A, A),
+        out_shape=(VM((D, D), f32), VM((96, 8, K), f32), VM((96, K), f32)),
+        in_specs=[pl.BlockSpec(memory_space=pltpu.SMEM), V, A, A, A, A],
+        out_specs=(V, V, V),
         scratch_shapes=[
-            VM((D, D), bf), VM((96, 8, K), bf), VM((D, D), f32), VM((96, 8, K), f32), VM((96, K), f32),
-            VM((D, R), bf), VM((G, R, 128), bf), VM((D, R), bf), VM((128, R), bf),
+            VM((R, D), bf), VM((K, D), bf), VM((D, D), bf), VM((96, 8, K), bf),
+            VM((R, D), bf), VM((G, R, 128), bf), VM((D, R), bf), VM((128, R), bf),
             T(G, 2, NA, 4), T(2, NA), T(G, NA, 4), T(NA),
             VM((G, NA, 48, 128), bf), VM((G, NA, 48, 128), bf), T(G, NZ, 5), T(G, 2, NA, 5),
-            DS((2,)), DS((2, G)), DS((G,)), DS((G,)), DS((1,)), DS((1,)), DS((G,)), DS((G,)),
+            DS((7,)), DS((G,)), DS((G,)), DS((1,)), DS((1,)), DS((G,)), DS((G,)),
             DS((G,)), DS((G,)), DS((G,)), DS((G,)), DS((G,)), DS((G,)),
-        ] + [VM((CH, K), bf)] * SLOTS,
-        compiler_params=pltpu.CompilerParams(vmem_limit_bytes=56 * 2**20, collective_id=0, has_side_effects=True),
+        ] + [VM((R, K), bf)] * SLOTS,
+        compiler_params=pltpu.CompilerParams(vmem_limit_bytes=VL * 2**20, collective_id=0, has_side_effects=True),
         cost_estimate=pl.CostEstimate(flops=2**34, bytes_accessed=2**23, transcendentals=2**24),
-    )(tiles, rows, cells, cent, rot, cb)
+    )(tiles, cells, rows, cent, rot, cb)
 
 
 def per_device(sample_rows, row_cell, tile_rows, centroids, rotation, codebooks):

time: 77.1 us -> 73.2 us (0.949)
  local copies, waits for them, and re-layouts: 4.83 us -> 2.93 us
  Pallas kernels: 71.4 us -> 69.6 us
    unnamed x7 -> x3, local copies, waits for them, and re-layouts: 4.83 us -> 2.93 us
    pallas_call x1, Pallas kernels: 71.4 us -> 69.6 us  [run(): pl.pallas_call(kernel, out_shape=(VM((D, D), f32), VM((96, 8, K), f32), V...]
where the time goes in v4:
time: 73.2 us; the launch traced here: 73.1 us
  Pallas kernels  69.6 us (95%)
  local copies, waits for them, and re-layouts  2.93 us (4%)
    pallas_call x1, Pallas kernels, run(): pl.pallas_call(kernel, out_shape=(VM((D, D), f32), VM((96, 8, K), f32), V...  69.6 us
    unnamed x3, local copies, waits for them, and re-layouts  2.93 us

profile of v4, /device:TPU:1, one launch (start us, length us, event | category | flops | bytes accessed | tf_op | source)
XLA Modules:
  0.0 73.1 jit_solution(9610480120691773420)
XLA Ops:
  0.6 69.6 %shard_map.85 = (f32[768,768]{1,0:T(8,128)S(1)}, f32[96,8,256]{2,1,0:T(8,128)S(1)}, f32[96,256]{1,0:T(8,128)S(1)}) custom-call(s32[2]{0:T(128)} %tiles.1, s32[8,128]{1,0:T(8,128)} %bitcast.1, bf16[1024,768]{1,0:T(8,128)(2,1)} %rows_hbm.1, bf16[256,768]{1,0:T(8,128)(2,1)} %cent_hbm.1, bf16[768,768]{1,0:T(8,128)(2,1)} %rot_hbm.1, bf16[96,8,256]{2,1,0:T(8,128)(2,1)} %cb_hbm.1), custom_call_target="tpu_custom_call" | custom-call | flops 17179869184 | bytes 8388608 | tf_op jit(solution)/shard_map/pallas_call | solution.py:263
  70.2 1.4 %copy.12 = f32[768,768]{1,0:T(8,128)} copy(f32[768,768]{1,0:T(8,128)S(1)} %get-tuple-element.3) | data formatting | bytes 4718592
  71.6 0.6 copy.14
  72.2 0.9 %copy.13 = f32[96,8,256]{2,1,0:T(8,128)} copy(f32[96,8,256]{2,1,0:T(8,128)S(1)} %get-tuple-element.4) | data formatting | bytes 1572864

commit v5 on v4

v5 whole, which is shorter than its diff:
```python
import functools
import jax
import jax.numpy as jnp
from jax import lax
from jax.sharding import PartitionSpec as P
import jax.experimental.pallas as pl
import jax.experimental.pallas.tpu as pltpu

bf = jnp.bfloat16
f32 = jnp.float32
LOG2E = 1.4426950408889634
NT = (((1,), (1,)), ((), ()))
TN = (((0,), (0,)), ((), ()))
MESH = pl.DeviceIdType.MESH
R = 1024
D = 768
K = 256
G = 6
GM = 16
CH = 256
NC = R // CH
CHB = 512
NCB = R // CHB
PB = CHB // CH
DB, DC, SLOTS = 6, 12, 8
U = GM * NC
Q = G + 1
NX, NY, NZ, NA = 4, 4, 8, 16
ROWS = 262144
VL = 52


def prep(rows, cells, base, cent, rot, rows_of, wait_rot, resid, yx, yT):
    for b in range(NC):
        rs = slice(b * 256, (b + 1) * 256)
        hot = [
            (lax.broadcasted_iota(jnp.int32, (K, 128), 0) + base == cells[b * 2 + i : b * 2 + i + 1, :]).astype(bf)
            for i in range(2)
        ]
        c = lax.dot_general(jnp.concatenate(hot, axis=1), cent[...], TN, preferred_element_type=f32)
        rows_of(b).wait()
        r = (rows[rs, :].astype(f32) - c).astype(bf)
        resid[rs, :] = r
        if b == 0:
            wait_rot()
        y = jnp.dot(r, rot[...], preferred_element_type=f32).astype(bf)
        yT[:, rs] = y.T
        for g in range(G):
            yx[g, rs, :] = y[:, g * 128 : (g + 1) * 128]


def scores(t, g, cb, yx, mats, slots):
    j, ch = divmod(t, NC)
    rs = slice(ch * CH, (ch + 1) * CH)
    if ch == 0:
        c = cb[g * GM + j].astype(f32)
        bias = -0.5 * jnp.sum(c * c, axis=0, keepdims=True)
        row = lax.broadcasted_iota(jnp.int32, (128, K), 0)
        mats[j] = (jnp.where(row // 8 == j, jnp.concatenate([c] * 16, axis=0), 0.0).astype(bf), bias)
    s = jnp.dot(yx[g, rs, :], mats[j][0], preferred_element_type=f32) + mats[j][1]
    s = s - jnp.max(s, axis=1, keepdims=True)
    slots[j % SLOTS][rs, :] = jnp.exp2(s * LOG2E).astype(bf)


def reconstruct(u, g, cb, yT, valid, slots, held, lhs, apT):
    j, ch = divmod(u, NCB)
    rs = slice(ch * CHB, (ch + 1) * CHB)
    one = (lax.broadcasted_iota(jnp.int32, (8, K), 0) == 0).astype(f32)
    mat = jnp.concatenate([cb[g * GM + j].astype(f32), one], axis=0).astype(bf)
    q = lax.dot_general(mat, slots[j % SLOTS][rs, :], NT, preferred_element_type=f32)
    inv = valid[:, rs] / q[8:9, :]
    r0 = pl.multiple_of(g * 128 + (j // 2) * 16, 16)
    y = yT[pl.ds(r0, 16), rs].astype(f32)[(j % 2) * 8 : (j % 2) * 8 + 8, :]
    row = lax.broadcasted_iota(jnp.int32, (8, CHB), 0)
    lhs[u % 8] = jnp.concatenate([y * inv, jnp.where(row == 0, inv, 0.0)], axis=0).astype(bf)
    if j % 2 == 0:
        held[ch] = q[0:8, :] * inv
    else:
        apT[(j // 2) * 16 : (j // 2) * 16 + 16, rs] = jnp.concatenate([held[ch], q[0:8, :] * inv], axis=0).astype(bf)


def accumulate(u, g, slots, lhs, acc, mrow, part, pm):
    j, ch = divmod(u, NCB)
    rs = slice(ch * CHB, (ch + 1) * CHB)
    o = jnp.dot(lhs[u % 8], slots[j % SLOTS][rs, :], preferred_element_type=f32)
    if ch == 0:
        acc[j % 2] = o
    else:
        o = acc[j % 2] + o
        cc, a = j // 8, (j % 8) * 2
        part[g, cc, a, 3] = o[0:8, 0:128]
        part[g, cc, a + 1, 3] = o[0:8, 128:256]
        mrow[j % 8 : j % 8 + 1, :] = o[8:9, :]
        if j % 8 == 7:
            pm[0, g * 2 + cc] = mrow[:, 0:128]
            pm[1, g * 2 + cc] = mrow[:, 128:256]


def covariance(g, resid, apT, part):
    v = jnp.dot(apT[...], resid[...], preferred_element_type=f32)
    for cc in range(2):
        part[g, cc, :, 0:3] = v[:, cc * 384 : cc * 384 + 384].T.reshape(NA, 3, 8, 128)


def half_group(e, resid, apT, part, ph):
    v = jnp.dot(apT[e * 64 : e * 64 + 64, :], resid[...], preferred_element_type=f32)
    v = jnp.concatenate([v[:, 0:384], v[:, 384:768]], axis=0).T
    for cc in range(2):
        ph[e, cc, 0:12] = v[cc * 192 : cc * 192 + 192].reshape(12, 2, 8, 128)
        for a in range(8):
            ph[e, cc, 12 + a // 2, a % 2] = part[G - 1, e, cc * 8 + a, 3]


def kernel(tiles, cells, rows_hbm, cent_hbm, rot_hbm, cb_hbm, cov, sums, mass,
           rows, cent, rot, cb, resid, yx, yT, apT, held, lhs, acc, mrow, part, ph, pm, rc, rcm, sa, ra, rz, out,
           s_in, s_core, r_core, s_m, r_m, s_a, r_a, s_z, r_z, s_g, r_g, s_c, r_c, *slots):
    grp = lax.axis_index("grp")
    dev = lax.axis_index("dev")
    yy = grp // 2
    c = lax.rem(grp, 2)
    zz = dev // NX
    xx = lax.rem(dev, NX)
    me = yy * NX + xx
    sib = (yy * 2 + 1 - c, dev)

    def plane(a):
        return ((a // NX) * 2 + c, zz * NX + lax.rem(a, NX))

    def column(z):
        return (grp, z * NX + xx)

    others = [lax.rem(me + k, NA) for k in range(1, NA)]
    above = [lax.rem(zz + k, NZ) for k in range(1, NZ)]
    def copy(src, dst, ss, rs, to):
        return pltpu.make_async_remote_copy(
            src_ref=src, dst_ref=dst, send_sem=ss, recv_sem=rs, device_id=to, device_id_type=MESH
        )

    def size(kind):
        return ((4, 4, 32), (2, 2, 16), (2, 3, 32))[kind]

    def step(k, q, kind=0):
        m, n, nb = size(kind)
        mine_of, from_sib = (part.at[q, c], part.at[q, 1 - c]) if kind == 0 else (ph.at[kind - 1, c], ph.at[kind - 1, 1 - c])
        got = rc.at[q, :, 0:m]
        if k == 0:
            copy(from_sib, got, s_core.at[q], r_core.at[q], sib).start()
            if kind == 2:
                copy(pm.at[1 - c], rcm, s_m.at[0], r_m.at[0], sib).start()
        if k == 1:
            copy(got, got, s_core.at[q], r_core.at[q], sib).wait_recv()
            if kind == 2:
                copy(rcm, rcm, s_m.at[0], r_m.at[0], sib).wait_recv()
                tot = (pm[c] + rcm[...]).reshape(NA, 8, 128)
                tot = jnp.concatenate([tot, jnp.zeros((NA, 8, 128), f32)], axis=1)
                sa[q, :, 16:32] = tot.astype(bf)
            sa[q, :, 0 : m * 8] = (mine_of[...] + got[...]).reshape(NA, m * 8, 128).astype(bf)
            for a in others:
                copy(sa.at[q, a, 0:nb], ra.at[q, me, 0:nb], s_a.at[q], r_a.at[q], plane(a)).start()
            ra[q, me, 0:nb] = sa[q, me, 0:nb]
        if k == 2:
            copy(sa.at[q, 0:15, 0:nb], ra.at[q, 0:15, 0:nb], s_a.at[q], r_a.at[q], sib).wait_recv()
            t = [ra[q, a, 0:nb].astype(f32) for a in range(NA)]
            while len(t) > 1:
                t = [t[i] + t[i + 1] for i in range(0, len(t), 2)]
            rz[q, zz, 0:n] = t[0][0 : n * 8].reshape(n, 8, 128)
            for z in above:
                copy(rz.at[q, zz, 0:n], rz.at[q, zz, 0:n], s_z.at[q], r_z.at[q], column(z)).start()
        if k == 3:
            copy(rz.at[q, 0:7, 0:n], rz.at[q, 0:7, 0:n], s_z.at[q], r_z.at[q], sib).wait_recv()
            t = [rz[q, z, 0:n] for z in range(NZ)]
            while len(t) > 1:
                t = [t[i] + t[i + 1] for i in range(0, len(t), 2)]
            mine = out.at[q, c, me, 0:n]
            mine[...] = t[0]
            for a in others:
                copy(mine, mine, s_g.at[q], r_g.at[q], plane(a)).start()
        if k == 4:
            copy(out.at[q, c, 0:15, 0:n], out.at[q, c, 0:15, 0:n], s_g.at[q], r_g.at[q], sib).wait_recv()
            half = out.at[q, c, :, 0:n]
            copy(half, half, s_c.at[q], r_c.at[q], sib).start()
            unpack(q, kind, c)
        if k == 5:
            half = out.at[q, 1 - c, :, 0:n]
            copy(half, half, s_c.at[q], r_c.at[q], sib).wait_recv()
            unpack(q, kind, 1 - c)

    def unpack(q, kind, cc):
        if kind == 0:
            v = out[q, cc, :, 0:3].reshape(384, 128) * (1.0 / ROWS)
            cov[pl.ds(pl.multiple_of(cc * 384, 8), 384), pl.ds(pl.multiple_of(q * 128, 128), 128)] = v
            for a in range(NA):
                w = a % 2
                sums[q * GM + cc * 8 + a // 2, :, w * 128 : (w + 1) * 128] = out[q, cc, a, 3] * (K / ROWS)
        else:
            for a in range(8):
                w = a % 2
                i = (G - 1) * GM + (kind - 1) * 8 + cc * 4 + a // 2
                sums[i, :, w * 128 : (w + 1) * 128] = out[q, cc, 12 + a // 2, w] * (K / ROWS)
        if kind == 2:
            i0 = cc * 192
            v0 = out[q - 1, cc, 0:12, 0:2].reshape(192, 128) * (1.0 / ROWS)
            v1 = out[q, cc, 0:12, 0:2].reshape(192, 128) * (1.0 / ROWS)
            low = lax.broadcasted_iota(jnp.int32, (192, 128), 1) < 64
            cov[pl.ds(pl.multiple_of(i0, 8), 192), 640:768] = jnp.where(low, v0, pltpu.roll(v1, 64, 1))
            cov[pl.ds(pl.multiple_of(384 + i0, 8), 192), 640:768] = jnp.where(low, pltpu.roll(v0, 64, 1), v1)
            for a in range(12):
                mass[a * 8 : a * 8 + 8, pl.ds(pl.multiple_of(cc * 128, 128), 128)] = out[q, cc, a, 2] * (K / ROWS)

    barrier = pltpu.get_barrier_semaphore()
    peers = [sib] + [plane(a) for a in others] + [column(z) for z in above]
    for p in peers:
        pl.semaphore_signal(barrier, inc=1, device_id=p, device_id_type=MESH)

    def rows_of(b):
        rs = slice(b * 256, (b + 1) * 256)
        return pltpu.make_async_copy(rows_hbm.at[rs], rows.at[rs], s_in.at[3 + b])

    get_cent = pltpu.make_async_copy(cent_hbm, cent, s_in.at[2])
    get_rot = pltpu.make_async_copy(rot_hbm, rot, s_in.at[0])
    get_cb = pltpu.make_async_copy(cb_hbm, cb, s_in.at[1])
    for cp in [get_cent, rows_of(0), get_rot] + [rows_of(b) for b in range(1, NC)] + [get_cb]:
        cp.start()
    pm[...] = jnp.zeros_like(pm)
    get_cent.wait()
    prep(rows, cells, (grp * (NX * NZ) + dev) * K, cent, rot, rows_of, get_rot.wait, resid, yx, yT)
    pos = lax.broadcasted_iota(jnp.int32, (1, R), 1)
    valid = (pos < jnp.where(pos < 512, tiles[0], 512 + tiles[1])).astype(f32)
    get_cb.wait()

    def when(g, back, k):
        @pl.when(g >= back)
        def _():
            step(k, g - back)

    def later(t, g, before):
        for lag, work in ((DB, recon), (DC, accum)):
            v = t - lag
            if v % PB == PB - 1 and (v < 0 or g is not None):
                work((v % U) // PB, before if v < 0 else g)

    def recon(u, g):
        reconstruct(u, g, cb, yT, valid, slots, held, lhs, apT)

    def accum(u, g):
        accumulate(u, g, slots, lhs, acc, mrow, part, pm)

    def body(g, _):
        before = jnp.maximum(g - 1, 0)
        mats = {}
        for t in range(U):
            scores(t, g, cb, yx, mats, slots)
            later(t, g, before)
            if t == DB:
                covariance(before, resid, apT, part)
            if t == DC:

                @pl.when(g >= 1)
                def _():
                    @pl.when(g == 1)
                    def _():
                        pl.semaphore_wait(barrier, len(peers))

                    step(0, g - 1)
                    when(g, 4, 3)

            if t == U // 2 + DC:

                @pl.when(g >= 1)
                def _():
                    step(1, g - 1)
                    when(g, 2, 2)

                    @pl.when(g == G - 1)
                    def _():
                        half_group(0, resid, apT, part, ph)
                        step(0, G - 1, 1)

        return 0

    lax.fori_loop(0, G, body, 0)
    step(1, 5, 1)
    for t in range(U, U + DC):
        later(t - U, None, G - 1)
    half_group(1, resid, apT, part, ph)
    step(0, 6, 2)
    order = (
        (1, 6), (3, 2), (2, 4), (2, 5), (2, 6), (3, 3), (3, 5), (3, 4), (3, 6), (4, 0), (5, 0), (4, 1), (5, 1),
        (4, 2), (5, 2), (4, 3), (5, 3), (4, 5), (4, 4), (5, 4), (5, 5), (4, 6), (5, 6),
    )
    for k, q in order:
        step(k, q, max(q - 4, 0))
    copy(rcm, rcm, s_m.at[0], r_m.at[0], sib).wait_send()
    for q in range(Q):
        m, n, nb = size(max(q - 4, 0))
        copy(rc.at[q, :, 0:m], rc.at[q, :, 0:m], s_core.at[q], r_core.at[q], sib).wait_send()
        copy(sa.at[q, 0:15, 0:nb], ra.at[q, 0:15, 0:nb], s_a.at[q], r_a.at[q], sib).wait_send()
        copy(rz.at[q, 0:7, 0:n], rz.at[q, 0:7, 0:n], s_z.at[q], r_z.at[q], sib).wait_send()
        copy(out.at[q, 0, 0:15, 0:n], out.at[q, 0, 0:15, 0:n], s_g.at[q], r_g.at[q], sib).wait_send()
        copy(out.at[q, 0, :, 0:n], out.at[q, 0, :, 0:n], s_c.at[q], r_c.at[q], sib).wait_send()


def run(tiles, rows, cells, cent, rot, cb):
    V = pl.BlockSpec(memory_space=pltpu.VMEM)
    A = pl.BlockSpec(memory_space=pltpu.HBM)
    VM = pltpu.VMEM
    DS = pltpu.SemaphoreType.DMA

    def T(*n):
        return VM(n + (8, 128), f32)

    return pl.pallas_call(
        kernel,
        out_shape=(VM((D, D), f32), VM((96, 8, K), f32), VM((96, K), f32)),
        in_specs=[pl.BlockSpec(memory_space=pltpu.SMEM), V, A, A, A, A],
        out_specs=(V, V, V),
        scratch_shapes=[
            VM((R, D), bf), VM((K, D), bf), VM((D, D), bf), VM((96, 8, K), bf),
            VM((R, D), bf), VM((G, R, 128), bf), VM((D, R), bf), VM((128, R), bf),
            VM((NCB, 8, CHB), f32), VM((8, 16, CHB), bf), VM((2, 16, K), f32), VM((8, K), f32),
            T(G, 2, NA, 4), T(2, 2, NA, 2), T(2, NA), T(Q, NA, 4), T(NA),
            VM((Q, NA, 32, 128), bf), VM((Q, NA, 32, 128), bf), T(Q, NZ, 4), T(Q, 2, NA, 4),
            DS((7,)), DS((Q,)), DS((Q,)), DS((1,)), DS((1,)), DS((Q,)), DS((Q,)),
            DS((Q,)), DS((Q,)), DS((Q,)), DS((Q,)), DS((Q,)), DS((Q,)),
        ] + [VM((R, K), bf)] * SLOTS,
        compiler_params=pltpu.CompilerParams(vmem_limit_bytes=VL * 2**20, collective_id=0, has_side_effects=True),
        cost_estimate=pl.CostEstimate(flops=2**34, bytes_accessed=2**23, transcendentals=2**24),
    )(tiles, cells, rows, cent, rot, cb)


def per_device(sample_rows, row_cell, tile_rows, centroids, rotation, codebooks):
    return run(tile_rows, sample_rows, row_cell.reshape(8, 128), centroids, rotation, codebooks)


def solution(mesh):
    placed = (P(("grp", "dev"), None), P(("grp", "dev")), P(("grp", "dev")), P(("grp", "dev"), None), P(), P())
    return jax.shard_map(
        per_device, mesh=mesh, in_specs=placed, out_specs=(P(), P(), P()), check_vma=False
    )
```

time: 73.2 us -> 72.2 us (0.986)
  Pallas kernels: 69.6 us -> 68.5 us
    pallas_call x1, Pallas kernels: 69.6 us -> 68.5 us  [run(): pl.pallas_call(kernel, out_shape=(VM((D, D), f32), VM((96, 8, K), f32), V...]
where the time goes in v5:
time: 72.2 us; the launch traced here: 72.1 us
  Pallas kernels  68.5 us (95%)
  local copies, waits for them, and re-layouts  2.93 us (4%)
    pallas_call x1, Pallas kernels, run(): pl.pallas_call(kernel, out_shape=(VM((D, D), f32), VM((96, 8, K), f32), V...  68.5 us
    unnamed x3, local copies, waits for them, and re-layouts  2.93 us

profile of v5, /device:TPU:1, one launch (start us, length us, event | category | flops | bytes accessed | tf_op | source)
XLA Modules:
  0.0 72.1 jit_solution(10365728358242185656)
XLA Ops:
  0.6 68.5 %shard_map.85 = (f32[768,768]{1,0:T(8,128)S(1)}, f32[96,8,256]{2,1,0:T(8,128)S(1)}, f32[96,256]{1,0:T(8,128)S(1)}) custom-call(s32[2]{0:T(128)} %tiles.1, s32[8,128]{1,0:T(8,128)} %bitcast.1, bf16[1024,768]{1,0:T(8,128)(2,1)} %rows_hbm.1, bf16[256,768]{1,0:T(8,128)(2,1)} %cent_hbm.1, bf16[768,768]{1,0:T(8,128)(2,1)} %rot_hbm.1, bf16[96,8,256]{2,1,0:T(8,128)(2,1)} %cb_hbm.1), custom_call_target="tpu_custom_call" | custom-call | flops 17179869184 | bytes 8388608 | tf_op jit(solution)/shard_map/pallas_call | solution.py:312
  69.1 1.4 %copy.12 = f32[768,768]{1,0:T(8,128)} copy(f32[768,768]{1,0:T(8,128)S(1)} %get-tuple-element.3) | data formatting | bytes 4718592
  70.5 0.6 copy.14
  71.2 0.9 %copy.13 = f32[96,8,256]{2,1,0:T(8,128)} copy(f32[96,8,256]{2,1,0:T(8,128)S(1)} %get-tuple-element.4) | data formatting | bytes 1572864
